TPU v7x, 32 devices: a whole 2x2x4 slice. The times are simulated.
32 devices in a mesh: row: 4 (over y, x), col: 8 (over z, core).
Axes of the slice: x: 2, y: 2, z: 4, core: 2. Of those that a mesh axis runs over, the one named last changes fastest.
Arguments:
- trunk: bfloat16 [1024, 256], P(('row', 'col')), may hold values from -6 to 6
- row_weight: bfloat16 [256, 512], replicated, may hold values from -0.375 to 0.375
- column_weight: bfloat16 [256, 512], replicated, may hold values from -0.375 to 0.375
- pair_map_weight: bfloat16 [512, 48], replicated, may hold values from -0.25 to 0.25
- dilated_weight: bfloat16 [3, 3, 48, 48], replicated, may hold values from -0.3125 to 0.3125
- mixing_weight: bfloat16 [48, 48], replicated, may hold values from -0.875 to 0.875
Outputs:
- block_out: bfloat16 [48, 1024, 1024], P(None, 'row', 'col')
All inputs are finite; a program needn't handle non-finite values.
Results may differ from a plain program's by a relative error of at most 0.0067.
Values may be sent and summed in bfloat16 or wider, within the bound.
No kernel may reach another device: no remote copies, remote signals or barrier semaphores. Data moves between devices by JAX's collectives and lax.ppermute only.
A program may use at most 128 MiB of HBM per device.

v0:
```python
import functools

import jax
import jax.numpy as jnp
from jax import lax
from jax.experimental import pallas as pl
from jax.experimental.pallas import tpu as pltpu
from jax.sharding import Mesh
from jax.sharding import PartitionSpec as P

STEP = 8
TILE = 2 * STEP
TAPS = 3
PART = 4
WINDOWS = TAPS + 2
GROUP = TAPS * STEP
OUTSIDE = -1e30


def kernel(
    n_row,
    n_chip,
    mine,
    other,
    weights,
    out,
    conv_weight,
    mix_weight,
    row_proj,
    col_proj,
    base,
    sides,
    result,
    staged,
    sems,
):
    depth = 2 * mine.shape[1]
    row_weight = weights.at[pl.ds(0, depth)]
    col_weight = weights.at[pl.ds(depth, depth)]
    pair_weight = weights.at[pl.ds(2 * depth, out.shape[0])]
    f32, bf16 = jnp.float32, jnp.bfloat16
    row, chip, core = (lax.axis_index(name) for name in ("row", "chip", "core"))
    channels, n_rows, n_cols = out.shape

    span = conv_weight.shape[1]

    def block(at):
        cells = weights[pl.ds(2 * depth + (1 + at) * channels, channels), :span]
        return cells.astype(f32)

    taps = [[block(a * TAPS + b) for b in range(TAPS)] for a in range(TAPS)]
    mixing = block(TAPS * TAPS)
    for m in range(TAPS):
        for b in range(TAPS):
            moved = [pltpu.roll(taps[a][b], (m + a) * channels, 1) for a in range(TAPS)]
            rows = pl.ds((b * TAPS + m) * channels, channels)
            conv_weight[rows, :] = (moved[0] + moved[1] + moved[2]).astype(bf16)
        moved = pltpu.roll(mixing, m * channels, 1) if m else mixing
        mix_weight[pl.ds(m * channels, channels), :] = moved.astype(bf16)

    tiles = n_cols // TILE + 1
    zero = jnp.zeros((), bf16)

    def projected(start, size, weight):
        ends = (jnp.maximum(start - TILE, 0), jnp.minimum(start + size, mine.shape[0] - TILE))
        spans = [pl.ds(pl.multiple_of(start, TILE), size)]
        spans += [pl.ds(pl.multiple_of(end, TILE), TILE) for end in ends]
        halves = [jnp.concatenate([half[rows] for rows in spans], axis=0) for half in (mine, other)]
        cells = jnp.concatenate(
            [jnp.where(core == k, halves[0], halves[1]) for k in range(2)], axis=1
        )
        cells = jnp.dot(cells, weight[...], preferred_element_type=f32).astype(bf16).astype(f32)
        return cells[:size], cells[size + STEP : size + TILE], cells[size + TILE : size + TILE + STEP]

    width = row_proj.shape[1]

    cells, left, right = projected((chip * 2 + core) * n_cols, n_cols, col_weight)
    col_proj[:n_cols, :] = cells.astype(bf16)
    left = jnp.where((chip == 0) & (core == 0), OUTSIDE, left)
    right = jnp.where((chip == n_chip - 1) & (core == 1), OUTSIDE, right)
    col_proj[n_cols:, :] = jnp.concatenate([right, left], axis=0).astype(bf16)

    cells, left, right = projected(row * n_rows, n_rows, row_weight)
    row_proj[:STEP, :] = jnp.where(row == 0, OUTSIDE, left)
    row_proj[STEP : STEP + n_rows, :] = cells
    row_proj[STEP + n_rows : TILE + n_rows, :] = jnp.where(row == n_row - 1, OUTSIDE, right)
    spare = row_proj.shape[0] - TILE - n_rows
    row_proj[TILE + n_rows :, :] = jnp.full((spare, width), OUTSIDE, f32)

    lane = lax.broadcasted_iota(jnp.int32, (1, n_cols), 1)
    transposed = (((1,), (1,)), ((), ()))

    def pair_cells(acts):
        act = jnp.concatenate(acts, axis=0)
        hidden = lax.dot_general(pair_weight[...], act, transposed, preferred_element_type=f32)
        return hidden.astype(bf16)

    def pair_rows(start, count, outer):
        rows = row_proj[pl.ds(pl.multiple_of(start, STEP), count), :]
        hidden = []
        for low in range(0, count, PART):
            inner = []
            for k in range(low, low + PART):
                spread = jnp.broadcast_to(rows[k : k + 1], (TILE, width)).astype(bf16)
                cells = col_proj[...].reshape(tiles, TILE, width) + spread[None]
                act = jnp.maximum(cells, zero)
                inner.append(act[:-1].reshape(n_cols, width))
                outer.append(act[-1])
            hidden.append(pair_cells(inner))
        return hidden

    def put_rows(start, hidden):
        for n, cells in enumerate(hidden):
            for k in range(PART):
                base[start + n * PART + k] = cells[:, k * n_cols : (k + 1) * n_cols]

    def put_sides(start, cells):
        for k in range(cells.shape[1] // n_cols):
            sides[start // STEP + k] = cells[:, k * n_cols : (k + 1) * n_cols]

    reach = TAPS * channels
    pitch = channels + STEP
    fill = [jnp.zeros((span - WINDOWS * channels, n_cols), bf16)]
    wide = (STEP + 1) * n_cols

    def conv_parts(groups):
        cells = []
        for at in groups:
            for p in range(STEP):
                windows = [base[at * GROUP + p + STEP * m] for m in range(WINDOWS)]
                cells.append(jnp.concatenate(windows + fill, axis=0))
            windows = [sides[at * TAPS + m] for m in range(WINDOWS)]
            cells.append(jnp.concatenate(windows + fill, axis=0))
        cells = jnp.maximum(jnp.concatenate(cells, axis=1), zero)
        return jnp.dot(conv_weight[...], cells, preferred_element_type=f32)

    def shifted(parts):
        mids = []
        for low in range(0, parts.shape[1], wide):
            ends = parts[:, low + STEP * n_cols : low + wide]
            ends = jnp.where(lane % TILE >= STEP, ends[:reach], ends[2 * reach :])
            for p in range(STEP):
                here = parts[:, low + p * n_cols : low + (p + 1) * n_cols]
                end = pltpu.roll(ends, (n_cols - STEP - p * TILE) % n_cols, 1)
                left = jnp.where(lane < STEP, end, pltpu.roll(here[:reach], STEP, 1))
                right = pltpu.roll(here[2 * reach :], n_cols - STEP, 1)
                right = jnp.where(lane >= n_cols - STEP, end, right)
                total = here[reach : 2 * reach] + left + right
                mids.append(jnp.maximum(total, 0.0).astype(bf16))
        return jnp.concatenate(mids, axis=1)

    def mixed_rows(groups, mid):
        mixed = jnp.dot(mix_weight[:, :reach], mid, preferred_element_type=f32)
        for n, at in enumerate(groups):
            for p in range(STEP):
                for m in range(TAPS):
                    row_at = at * GROUP + p + STEP * m
                    low = (n * STEP + p) * n_cols
                    here = mixed[m * channels : (m + 1) * channels, low : low + n_cols]
                    here = here + base[row_at + STEP].astype(f32)
                    result[pl.ds(pl.multiple_of(row_at * pitch, STEP), channels), :] = here

    def turn_rows(start, count):
        start = pl.multiple_of(start, TILE)
        for o in range(channels):
            cells = result[pl.ds(start * pitch + o, count, stride=pitch), :]
            staged[o, pl.ds(start, count), :] = cells.astype(bf16)

    def to_out(start, count, sem):
        rows = pl.ds(pl.multiple_of(start, TILE), count)
        return pltpu.make_async_copy(staged.at[:, rows], out.at[:, rows], sem)

    per_step = 2 * GROUP
    steps = n_rows // per_step - 1
    ahead = per_step + TILE
    outer = []
    put_rows(0, pair_rows(0, ahead, outer))
    put_sides(0, pair_cells(outer))

    def step(at, _):
        groups = (2 * at, 2 * at + 1)
        start = at * per_step + ahead
        before = jnp.maximum(at - 1, 0)
        parts = conv_parts(groups)
        outer = []
        one = pair_rows(start, GROUP, outer)
        mid = shifted(parts)
        two = pair_rows(start + GROUP, GROUP, outer)
        outer = pair_cells(outer)
        turn_rows(before * per_step, per_step)
        mixed_rows(groups, mid)
        put_rows(start, one + two)
        put_sides(start, outer)

        @pl.when(at > 0)
        def _send():
            to_out(before * per_step, per_step, sems.at[before]).start()

        return _

    lax.fori_loop(0, steps, step, 0)
    done = steps * per_step
    groups = tuple(range(2 * steps, -(-n_rows // GROUP)))
    parts = conv_parts(groups[:2])
    outer = []
    hidden = pair_rows(done + ahead, GROUP, outer)
    outer = pair_cells(outer)
    turn_rows(done - per_step, per_step)
    to_out(done - per_step, per_step, sems.at[steps - 1]).start()
    mid = shifted(parts)
    put_rows(done + ahead, hidden)
    put_sides(done + ahead, outer)
    parts = conv_parts(groups[2:])
    mixed_rows(groups[:2], mid)
    mixed_rows(groups[2:], shifted(parts))
    turn_rows(done, n_rows - done)
    last = to_out(done, n_rows - done, sems.at[steps])
    last.start()
    for at in range(steps):
        to_out(at * per_step, per_step, sems.at[at]).wait()
    last.wait()


def on_device(trunk, row_weight, column_weight, pair_map_weight, dilated_weight, mixing_weight):
    n_row, n_chip = lax.axis_size("row"), lax.axis_size("chip")
    shard, depth = trunk.shape
    n_rows, n_cols = shard * n_chip * 2, shard * n_row
    channels = pair_map_weight.shape[1]
    width = row_weight.shape[1]
    small = jnp.concatenate([dilated_weight.reshape(-1, channels), mixing_weight], axis=0)
    small = jnp.pad(small, ((0, 0), (0, width - channels)))
    weights = jnp.concatenate([row_weight, column_weight, pair_map_weight.T, small], axis=0)

    half = depth // 2
    to = lax.broadcasted_iota(jnp.int32, (n_row * n_chip * 2, shard, half), 0)
    copies = jnp.where(to % 2 == 0, trunk[None, :, :half], trunk[None, :, half:])
    mine = lax.all_to_all(copies, ("row", "chip", "core"), 0, 0).reshape(-1, half)
    other = lax.ppermute(mine, "core", [(0, 1), (1, 0)])
    span = -(-WINDOWS * channels // n_cols) * n_cols
    groups = -(-n_rows // GROUP)
    padded = groups * GROUP + TILE
    return pl.pallas_call(
        functools.partial(kernel, n_row, n_chip),
        out_shape=jax.ShapeDtypeStruct((channels, n_rows, n_cols), jnp.bfloat16),
        out_specs=pl.BlockSpec(memory_space=pl.ANY),
        scratch_shapes=[
            pltpu.VMEM((TAPS * TAPS * channels, span), jnp.bfloat16),
            pltpu.VMEM((TAPS * channels, span), jnp.bfloat16),
            pltpu.VMEM((padded, width), jnp.float32),
            pltpu.VMEM((n_cols + TILE, width), jnp.bfloat16),
            pltpu.VMEM((padded, channels, n_cols), jnp.bfloat16),
            pltpu.VMEM((padded // STEP, channels, n_cols), jnp.bfloat16),
            pltpu.VMEM((groups * GROUP * (channels + STEP), n_cols), jnp.float32),
            pltpu.VMEM((channels, n_rows, n_cols), jnp.bfloat16),
            pltpu.SemaphoreType.DMA((n_rows // (2 * GROUP),)),
        ],
        compiler_params=pltpu.CompilerParams(vmem_limit_bytes=52 * 2**20),
        name="pair_block",
    )(mine, other, weights)


def solution(mesh):
    n_row, n_col = mesh.devices.shape
    chips = Mesh(mesh.devices.reshape(n_row, n_col // 2, 2), ("row", "chip", "core"))
    return jax.shard_map(
        on_device,
        mesh=chips,
        in_specs=(P(("row", "chip", "core"), None), P(), P(), P(), P(), P()),
        out_specs=P(None, "row", ("chip", "core")),
        check_vma=False,
    )
```

profile of v0, /device:TPU:0, one launch (start us, length us, event | category | flops | bytes accessed | tf_op | source)
XLA Modules:
  0.0 40.0 jit_solution(13394823759108610405)
XLA Ops:
  0.0 0.7 %fusion.4 = (bf16[32,128]{1,0:T(8,128)(2,1)S(1)}, bf16[32,128]{1,0:T(8,128)(2,1)S(1)}) fusion(bf16[32,256]{1,0:T(8,128)(2,1)} %param.6), kind=kLoop, calls=%fused_computation.10 | loop fusion | bytes 32768 | tf_op jit(solution)/shard_map/slice | solution.py:236
  0.7 0.9 %fusion.2 = bf16[32,32,128]{2,1,0:T(8,128)(2,1)} fusion(s32[32]{0:T(128)S(1)} %get-tuple-element.7, s32[32]{0:T(128)S(1)} %get-tuple-element.8, pred[32]{0:T(512)(128)(4,1)S(1)} %compare_and_fusion, bf16[32,128]{1,0:T(8,128)(2,1)S(1)} %get-tuple-element.6, bf16[32,128]{1,0:T(8,128)(2,1)S(1)} %get-tuple-element.5), kind=kLoop, calls=%fused_computation.5 | loop fusion | flops 393216 | bytes 278816 | tf_op jit(solution)/shard_map/jit(_where)/select_n | solution.py:236
  1.6 7.3 %all-to-all-start = ((bf16[32,32,128]{2,1,0:T(8,128)(2,1)}), bf16[32,32,128]{2,1,0:T(8,128)(2,1)S(1)}, u32[]{:S(2)}, u32[]{:S(2)}) async-start(bf16[32,32,128]{2,1,0:T(8,128)(2,1)} %fusion.2), calls=%async_computation | async-start | bytes 524288 | tf_op jit(solution)/shard_map/all_to_all | solution.py:237
  8.9 1.0 %fusion.3 = bf16[480,512]{1,0:T(8,128)(2,1)S(1)} fusion(bf16[48,48]{1,0:T(8,128)(2,1)} %param.11, bf16[432,48]{1,0:T(8,128)(2,1)} %bitcast.5), kind=kLoop, calls=%fused_computation.6 | loop fusion | flops 1720320 | bytes 537600 | tf_op jit(solution)/shard_map/concatenate | solution.py:230
  9.9 9.4 %all-to-all-done = bf16[32,32,128]{2,1,0:T(8,128)(2,1)S(1)} async-done(((bf16[32,32,128]{2,1,0:T(8,128)(2,1)}), bf16[32,32,128]{2,1,0:T(8,128)(2,1)S(1)}, u32[]{:S(2)}, u32[]{:S(2)}) %all-to-all-start) | async-done | bytes 262176 | tf_op jit(solution)/shard_map/all_to_all | solution.py:237
  19.3 0.4 collective-permute-start
  19.7 1.1 %pad_maximum_fusion.weights = bf16[1040,512]{1,0:T(8,128)(2,1)S(1)} fusion(bf16[480,512]{1,0:T(8,128)(2,1)S(1)} %fusion.3, bf16[48,512]{1,0:T(8,128)(2,1)} %bitcast.6, bf16[256,512]{1,0:T(8,128)(2,1)} %param.8, bf16[256,512]{1,0:T(8,128)(2,1)} %param.7), kind=kLoop, calls=%fused_computation | loop fusion | flops 4259840 | bytes 2129920 | tf_op jit(solution)/shard_map/concatenate | solution.py:232
  20.8 0.0 collective-permute-done.other
  20.8 19.1 %pair_block.1 = bf16[48,256,128]{2,1,0:T(8,128)(2,1)} custom-call(bf16[1024,128]{1,0:T(8,128)(2,1)S(1)} %bitcast.4, bf16[1024,128]{1,0:T(8,128)(2,1)S(1)} %collective-permute-done.other, bf16[1040,512]{1,0:T(8,128)(2,1)S(1)} %pad_maximum_fusion.weights), custom_call_target="tpu_custom_call" | custom-call | tf_op jit(solution)/shard_map/pair_block/pallas_call | solution.py:242
  (2 shorter events, 0.0 us)
Async XLA Ops:
  1.6 17.7 %all-to-all-start = ((bf16[32,32,128]{2,1,0:T(8,128)(2,1)}), bf16[32,32,128]{2,1,0:T(8,128)(2,1)S(1)}, u32[]{:S(2)}, u32[]{:S(2)}) async-start(bf16[32,32,128]{2,1,0:T(8,128)(2,1)} %fusion.2), calls=%async_computation | async-start | bytes 524288 | tf_op jit(solution)/shard_map/all_to_all | solution.py:237
  19.3 1.5 %collective-permute-start = (bf16[1024,128]{1,0:T(8,128)(2,1)S(1)}, bf16[1024,128]{1,0:T(8,128)(2,1)S(1)}, u32[]{:S(2)}, u32[]{:S(2)}) collective-permute-start(bf16[1024,128]{1,0:T(8,128)(2,1)S(1)} %bitcast.3), channel_id=1, source_target_pairs={{0,1},{1,0},{2,3},{3,2},{4,5},{5,4},{6,7},{7,6},{8,9},{9,8},{10,11... | collective-permute-start | bytes 786440 | tf_op jit(solution)/shard_map/ppermute | solution.py:238
where the time goes:
time: 40.3 us; the launch traced here: 40 us
  Pallas kernels  19.1 us (47%)
  waiting for transfers between devices  9.45 us (23%)
  starting transfers between devices  7.69 us (19%)
  other arithmetic  2.97 us (7%)
  local copies, waits for them, and re-layouts  0.72 us (2%)
    pallas_call x1, Pallas kernels, on_device(): pl.pallas_call(functools.partial(kernel, n_row, n_chip), out_shape=jax.Sh...  19.1 us
    all_to_all x1, waiting for transfers between devices, on_device(): lax.all_to_all(copies, ('row', 'chip', 'core'), 0, 0).reshape(-1, half)  9.42 us
    all_to_all x1, starting transfers between devices, on_device(): lax.all_to_all(copies, ('row', 'chip', 'core'), 0, 0).reshape(-1, half)  7.3 us
    concatenate x1, other arithmetic, on_device(): jnp.concatenate([row_weight, column_weight, pair_map_weight.T, small], ax...  1.13 us
    concatenate x1, other arithmetic, on_device(): jnp.concatenate([dilated_weight.reshape(-1, channels), mixing_weight], ax...  0.96 us
    select_n x1, other arithmetic, on_device(): jnp.where(to % 2 == 0, trunk[None, :, :half], trunk[None, :, half:])  0.87 us
  transfers between devices with their start and end apart: 2, of which 1 were waited for; matrix products, arithmetic and copies ran while one was open for 5% of the time, Pallas kernels for 0%

commit v1 on v0

--- a/solution.py
+++ b/solution.py
@@ -95,10 +95,9 @@
         hidden = lax.dot_general(pair_weight[...], act, transposed, preferred_element_type=f32)
         return hidden.astype(bf16)
 
-    def pair_rows(start, count, outer):
-        rows = row_proj[pl.ds(pl.multiple_of(start, STEP), count), :]
+    def pair_rows(rows, outer):
         hidden = []
-        for low in range(0, count, PART):
+        for low in range(0, rows.shape[0], PART):
             inner = []
             for k in range(low, low + PART):
                 spread = jnp.broadcast_to(rows[k : k + 1], (TILE, width)).astype(bf16)
@@ -121,44 +120,44 @@
     reach = TAPS * channels
     pitch = channels + STEP
     fill = [jnp.zeros((span - WINDOWS * channels, n_cols), bf16)]
-    wide = (STEP + 1) * n_cols
-
-    def conv_parts(groups):
-        cells = []
-        for at in groups:
-            for p in range(STEP):
-                windows = [base[at * GROUP + p + STEP * m] for m in range(WINDOWS)]
-                cells.append(jnp.concatenate(windows + fill, axis=0))
-            windows = [sides[at * TAPS + m] for m in range(WINDOWS)]
-            cells.append(jnp.concatenate(windows + fill, axis=0))
+
+    def conv_cells(blocks):
+        cells = [jnp.concatenate(windows + fill, axis=0) for windows in blocks]
         cells = jnp.maximum(jnp.concatenate(cells, axis=1), zero)
         return jnp.dot(conv_weight[...], cells, preferred_element_type=f32)
 
-    def shifted(parts):
+    def conv_ends(groups):
+        parts = conv_cells([[sides[at * TAPS + m] for m in range(WINDOWS)] for at in groups])
+        ends = []
+        for n in range(len(groups)):
+            part = parts[:, n * n_cols : (n + 1) * n_cols]
+            ends.append(jnp.where(lane % TILE >= STEP, part[:reach], part[2 * reach :]))
+        return ends
+
+    def conv_parts(at, low):
+        places = [at * GROUP + p for p in range(low, low + PART)]
+        return conv_cells([[base[p + STEP * m] for m in range(WINDOWS)] for p in places])
+
+    def shifted(parts, ends, low):
         mids = []
-        for low in range(0, parts.shape[1], wide):
-            ends = parts[:, low + STEP * n_cols : low + wide]
-            ends = jnp.where(lane % TILE >= STEP, ends[:reach], ends[2 * reach :])
-            for p in range(STEP):
-                here = parts[:, low + p * n_cols : low + (p + 1) * n_cols]
-                end = pltpu.roll(ends, (n_cols - STEP - p * TILE) % n_cols, 1)
-                left = jnp.where(lane < STEP, end, pltpu.roll(here[:reach], STEP, 1))
-                right = pltpu.roll(here[2 * reach :], n_cols - STEP, 1)
-                right = jnp.where(lane >= n_cols - STEP, end, right)
-                total = here[reach : 2 * reach] + left + right
-                mids.append(jnp.maximum(total, 0.0).astype(bf16))
+        for k in range(PART):
+            here = parts[:, k * n_cols : (k + 1) * n_cols]
+            end = pltpu.roll(ends, (n_cols - STEP - (low + k) * TILE) % n_cols, 1)
+            left = jnp.where(lane < STEP, end, pltpu.roll(here[:reach], STEP, 1))
+            right = pltpu.roll(here[2 * reach :], n_cols - STEP, 1)
+            right = jnp.where(lane >= n_cols - STEP, end, right)
+            total = here[reach : 2 * reach] + left + right
+            mids.append(jnp.maximum(total, 0.0).astype(bf16))
         return jnp.concatenate(mids, axis=1)
 
-    def mixed_rows(groups, mid):
+    def mixed_rows(at, low, mid):
         mixed = jnp.dot(mix_weight[:, :reach], mid, preferred_element_type=f32)
-        for n, at in enumerate(groups):
-            for p in range(STEP):
-                for m in range(TAPS):
-                    row_at = at * GROUP + p + STEP * m
-                    low = (n * STEP + p) * n_cols
-                    here = mixed[m * channels : (m + 1) * channels, low : low + n_cols]
-                    here = here + base[row_at + STEP].astype(f32)
-                    result[pl.ds(pl.multiple_of(row_at * pitch, STEP), channels), :] = here
+        for k in range(PART):
+            for m in range(TAPS):
+                row_at = at * GROUP + low + k + STEP * m
+                here = mixed[m * channels : (m + 1) * channels, k * n_cols : (k + 1) * n_cols]
+                here = here + base[row_at + STEP].astype(f32)
+                result[pl.ds(pl.multiple_of(row_at * pitch, STEP), channels), :] = here
 
     def turn_rows(start, count):
         start = pl.multiple_of(start, TILE)
@@ -174,23 +173,36 @@
     steps = n_rows // per_step - 1
     ahead = per_step + TILE
     outer = []
-    put_rows(0, pair_rows(0, ahead, outer))
+    put_rows(0, pair_rows(row_proj[:ahead, :], outer))
     put_sides(0, pair_cells(outer))
 
+    def rounds(groups, start, count, turn):
+        ends = conv_ends(groups)
+        places = [(n, low) for n in range(len(groups)) for low in range(0, STEP, PART)]
+        share = -(-count // (PART * len(places))) * PART
+        hidden, outer, mid = [], [], None
+        rows = row_proj[pl.ds(pl.multiple_of(start, STEP), count), :]
+        for n, (group, low) in enumerate(places):
+            parts = conv_parts(groups[group], low)
+            if n == 0:
+                turn()
+            hidden += pair_rows(rows[n * share : (n + 1) * share], outer)
+            if n:
+                mixed_rows(groups[places[n - 1][0]], places[n - 1][1], mid)
+            mid = shifted(parts, ends[group], low)
+        outer = pair_cells(outer)
+        mixed_rows(groups[-1], places[-1][1], mid)
+        put_rows(start, hidden)
+        put_sides(start, outer)
+
     def step(at, _):
-        groups = (2 * at, 2 * at + 1)
-        start = at * per_step + ahead
         before = jnp.maximum(at - 1, 0)
-        parts = conv_parts(groups)
-        outer = []
-        one = pair_rows(start, GROUP, outer)
-        mid = shifted(parts)
-        two = pair_rows(start + GROUP, GROUP, outer)
-        outer = pair_cells(outer)
-        turn_rows(before * per_step, per_step)
-        mixed_rows(groups, mid)
-        put_rows(start, one + two)
-        put_sides(start, outer)
+        rounds(
+            (2 * at, 2 * at + 1),
+            at * per_step + ahead,
+            per_step,
+            lambda: turn_rows(before * per_step, per_step),
+        )
 
         @pl.when(at > 0)
         def _send():
@@ -200,19 +212,18 @@
 
     lax.fori_loop(0, steps, step, 0)
     done = steps * per_step
-    groups = tuple(range(2 * steps, -(-n_rows // GROUP)))
-    parts = conv_parts(groups[:2])
-    outer = []
-    hidden = pair_rows(done + ahead, GROUP, outer)
-    outer = pair_cells(outer)
-    turn_rows(done - per_step, per_step)
+    rounds(
+        (2 * steps, 2 * steps + 1),
+        done + ahead,
+        GROUP,
+        lambda: turn_rows(done - per_step, per_step),
+    )
     to_out(done - per_step, per_step, sems.at[steps - 1]).start()
-    mid = shifted(parts)
-    put_rows(done + ahead, hidden)
-    put_sides(done + ahead, outer)
-    parts = conv_parts(groups[2:])
-    mixed_rows(groups[:2], mid)
-    mixed_rows(groups[2:], shifted(parts))
+    for at in range(2 * steps + 2, -(-n_rows // GROUP)):
+        (ends,) = conv_ends((at,))
+        mids = [(low, shifted(conv_parts(at, low), ends, low)) for low in range(0, STEP, PART)]
+        for low, mid in mids:
+            mixed_rows(at, low, mid)
     turn_rows(done, n_rows - done)
     last = to_out(done, n_rows - done, sems.at[steps])
     last.start()

time: 40.3 us -> 39.9 us (0.990)
  no operation moved by 1% of the time
where the time goes in v1:
time: 39.9 us; the launch traced here: 39.6 us
  Pallas kernels  18.8 us (47%)
  waiting for transfers between devices  9.45 us (24%)
  starting transfers between devices  7.69 us (19%)
  other arithmetic  2.97 us (7%)
  local copies, waits for them, and re-layouts  0.72 us (2%)
    pallas_call x1, Pallas kernels, on_device(): pl.pallas_call(functools.partial(kernel, n_row, n_chip), out_shape=jax.Sh...  18.8 us
    all_to_all x1, waiting for transfers between devices, on_device(): lax.all_to_all(copies, ('row', 'chip', 'core'), 0, 0).reshape(-1, half)  9.42 us
    all_to_all x1, starting transfers between devices, on_device(): lax.all_to_all(copies, ('row', 'chip', 'core'), 0, 0).reshape(-1, half)  7.3 us
    concatenate x1, other arithmetic, on_device(): jnp.concatenate([row_weight, column_weight, pair_map_weight.T, small], ax...  1.13 us
    concatenate x1, other arithmetic, on_device(): jnp.concatenate([dilated_weight.reshape(-1, channels), mixing_weight], ax...  0.96 us
    select_n x1, other arithmetic, on_device(): jnp.where(to % 2 == 0, trunk[None, :, :half], trunk[None, :, half:])  0.87 us
  transfers between devices with their start and end apart: 2, of which 1 were waited for; matrix products, arithmetic and copies ran while one was open for 5% of the time, Pallas kernels for 0%

profile of v1, /device:TPU:0, one launch (start us, length us, event | category | flops | bytes accessed | tf_op | source)
XLA Modules:
  0.0 39.6 jit_solution(5846926189492077443)
XLA Ops:
  0.0 0.7 %fusion.4 = (bf16[32,128]{1,0:T(8,128)(2,1)S(1)}, bf16[32,128]{1,0:T(8,128)(2,1)S(1)}) fusion(bf16[32,256]{1,0:T(8,128)(2,1)} %param.6), kind=kLoop, calls=%fused_computation.10 | loop fusion | bytes 32768 | tf_op jit(solution)/shard_map/slice | solution.py:247
  0.7 0.9 %fusion.2 = bf16[32,32,128]{2,1,0:T(8,128)(2,1)} fusion(s32[32]{0:T(128)S(1)} %get-tuple-element.7, s32[32]{0:T(128)S(1)} %get-tuple-element.8, pred[32]{0:T(512)(128)(4,1)S(1)} %compare_and_fusion, bf16[32,128]{1,0:T(8,128)(2,1)S(1)} %get-tuple-element.6, bf16[32,128]{1,0:T(8,128)(2,1)S(1)} %get-tuple-element.5), kind=kLoop, calls=%fused_computation.5 | loop fusion | flops 393216 | bytes 278816 | tf_op jit(solution)/shard_map/jit(_where)/select_n | solution.py:247
  1.6 7.3 %all-to-all-start = ((bf16[32,32,128]{2,1,0:T(8,128)(2,1)}), bf16[32,32,128]{2,1,0:T(8,128)(2,1)S(1)}, u32[]{:S(2)}, u32[]{:S(2)}) async-start(bf16[32,32,128]{2,1,0:T(8,128)(2,1)} %fusion.2), calls=%async_computation | async-start | bytes 524288 | tf_op jit(solution)/shard_map/all_to_all | solution.py:248
  8.9 1.0 %fusion.3 = bf16[480,512]{1,0:T(8,128)(2,1)S(1)} fusion(bf16[48,48]{1,0:T(8,128)(2,1)} %param.11, bf16[432,48]{1,0:T(8,128)(2,1)} %bitcast.5), kind=kLoop, calls=%fused_computation.6 | loop fusion | flops 1720320 | bytes 537600 | tf_op jit(solution)/shard_map/concatenate | solution.py:241
  9.9 9.4 %all-to-all-done = bf16[32,32,128]{2,1,0:T(8,128)(2,1)S(1)} async-done(((bf16[32,32,128]{2,1,0:T(8,128)(2,1)}), bf16[32,32,128]{2,1,0:T(8,128)(2,1)S(1)}, u32[]{:S(2)}, u32[]{:S(2)}) %all-to-all-start) | async-done | bytes 262176 | tf_op jit(solution)/shard_map/all_to_all | solution.py:248
  19.3 0.4 collective-permute-start
  19.7 1.1 %pad_maximum_fusion.weights = bf16[1040,512]{1,0:T(8,128)(2,1)S(1)} fusion(bf16[480,512]{1,0:T(8,128)(2,1)S(1)} %fusion.3, bf16[48,512]{1,0:T(8,128)(2,1)} %bitcast.6, bf16[256,512]{1,0:T(8,128)(2,1)} %param.8, bf16[256,512]{1,0:T(8,128)(2,1)} %param.7), kind=kLoop, calls=%fused_computation | loop fusion | flops 4259840 | bytes 2129920 | tf_op jit(solution)/shard_map/concatenate | solution.py:243
  20.8 0.0 collective-permute-done.other
  20.8 18.8 %pair_block.1 = bf16[48,256,128]{2,1,0:T(8,128)(2,1)} custom-call(bf16[1024,128]{1,0:T(8,128)(2,1)S(1)} %bitcast.4, bf16[1024,128]{1,0:T(8,128)(2,1)S(1)} %collective-permute-done.other, bf16[1040,512]{1,0:T(8,128)(2,1)S(1)} %pad_maximum_fusion.weights), custom_call_target="tpu_custom_call" | custom-call | tf_op jit(solution)/shard_map/pair_block/pallas_call | solution.py:253
  (2 shorter events, 0.0 us)
Async XLA Ops:
  1.6 17.7 %all-to-all-start = ((bf16[32,32,128]{2,1,0:T(8,128)(2,1)}), bf16[32,32,128]{2,1,0:T(8,128)(2,1)S(1)}, u32[]{:S(2)}, u32[]{:S(2)}) async-start(bf16[32,32,128]{2,1,0:T(8,128)(2,1)} %fusion.2), calls=%async_computation | async-start | bytes 524288 | tf_op jit(solution)/shard_map/all_to_all | solution.py:248
  19.3 1.5 %collective-permute-start = (bf16[1024,128]{1,0:T(8,128)(2,1)S(1)}, bf16[1024,128]{1,0:T(8,128)(2,1)S(1)}, u32[]{:S(2)}, u32[]{:S(2)}) collective-permute-start(bf16[1024,128]{1,0:T(8,128)(2,1)S(1)} %bitcast.3), channel_id=1, source_target_pairs={{0,1},{1,0},{2,3},{3,2},{4,5},{5,4},{6,7},{7,6},{8,9},{9,8},{10,11... | collective-permute-start | bytes 786440 | tf_op jit(solution)/shard_map/ppermute | solution.py:249

commit v2 on v1

--- a/solution.py
+++ b/solution.py
@@ -84,8 +84,6 @@
     row_proj[:STEP, :] = jnp.where(row == 0, OUTSIDE, left)
     row_proj[STEP : STEP + n_rows, :] = cells
     row_proj[STEP + n_rows : TILE + n_rows, :] = jnp.where(row == n_row - 1, OUTSIDE, right)
-    spare = row_proj.shape[0] - TILE - n_rows
-    row_proj[TILE + n_rows :, :] = jnp.full((spare, width), OUTSIDE, f32)
 
     lane = lax.broadcasted_iota(jnp.int32, (1, n_cols), 1)
     transposed = (((1,), (1,)), ((), ()))
@@ -210,24 +208,32 @@
 
         return _
 
+    spare = pl.ds(n_rows + TILE, STEP)
+    base[spare] = jnp.zeros_like(base[spare])
+    sides[(n_rows + TILE) // STEP] = jnp.zeros_like(sides[0])
     lax.fori_loop(0, steps, step, 0)
+
     done = steps * per_step
     rounds(
         (2 * steps, 2 * steps + 1),
         done + ahead,
-        GROUP,
+        TILE,
         lambda: turn_rows(done - per_step, per_step),
     )
     to_out(done - per_step, per_step, sems.at[steps - 1]).start()
-    for at in range(2 * steps + 2, -(-n_rows // GROUP)):
-        (ends,) = conv_ends((at,))
-        mids = [(low, shifted(conv_parts(at, low), ends, low)) for low in range(0, STEP, PART)]
-        for low, mid in mids:
-            mixed_rows(at, low, mid)
+    at = 2 * steps + 2
+    (ends,) = conv_ends((at,))
+    lows = range(0, STEP, PART)
+    parts = [conv_parts(at, low) for low in lows]
+    turn_rows(done, per_step)
+    to_out(done, per_step, sems.at[steps]).start()
+    for low, part in zip(lows, parts):
+        mixed_rows(at, low, shifted(part, ends, low))
+    done += per_step
     turn_rows(done, n_rows - done)
-    last = to_out(done, n_rows - done, sems.at[steps])
+    last = to_out(done, n_rows - done, sems.at[steps + 1])
     last.start()
-    for at in range(steps):
+    for at in range(steps + 1):
         to_out(at * per_step, per_step, sems.at[at]).wait()
     last.wait()
 
@@ -257,13 +263,13 @@
         scratch_shapes=[
             pltpu.VMEM((TAPS * TAPS * channels, span), jnp.bfloat16),
             pltpu.VMEM((TAPS * channels, span), jnp.bfloat16),
-            pltpu.VMEM((padded, width), jnp.float32),
+            pltpu.VMEM((n_rows + TILE, width), jnp.float32),
             pltpu.VMEM((n_cols + TILE, width), jnp.bfloat16),
             pltpu.VMEM((padded, channels, n_cols), jnp.bfloat16),
             pltpu.VMEM((padded // STEP, channels, n_cols), jnp.bfloat16),
             pltpu.VMEM((groups * GROUP * (channels + STEP), n_cols), jnp.float32),
             pltpu.VMEM((channels, n_rows, n_cols), jnp.bfloat16),
-            pltpu.SemaphoreType.DMA((n_rows // (2 * GROUP),)),
+            pltpu.SemaphoreType.DMA((n_rows // (2 * GROUP) + 1,)),
         ],
         compiler_params=pltpu.CompilerParams(vmem_limit_bytes=52 * 2**20),
         name="pair_block",

time: 39.9 us -> 39.4 us (0.987)
  Pallas kernels: 18.8 us -> 18.3 us
    pallas_call x1, Pallas kernels: 18.8 us -> 18.3 us  [on_device(): pl.pallas_call(functools.partial(kernel, n_row, n_chip), out_shape=jax.Sh...]
where the time goes in v2:
time: 39.4 us; the launch traced here: 39.1 us
  Pallas kernels  18.3 us (46%)
  waiting for transfers between devices  9.45 us (24%)
  starting transfers between devices  7.69 us (20%)
  other arithmetic  2.97 us (8%)
  local copies, waits for them, and re-layouts  0.72 us (2%)
    pallas_call x1, Pallas kernels, on_device(): pl.pallas_call(functools.partial(kernel, n_row, n_chip), out_shape=jax.Sh...  18.3 us
    all_to_all x1, waiting for transfers between devices, on_device(): lax.all_to_all(copies, ('row', 'chip', 'core'), 0, 0).reshape(-1, half)  9.42 us
    all_to_all x1, starting transfers between devices, on_device(): lax.all_to_all(copies, ('row', 'chip', 'core'), 0, 0).reshape(-1, half)  7.3 us
    concatenate x1, other arithmetic, on_device(): jnp.concatenate([row_weight, column_weight, pair_map_weight.T, small], ax...  1.13 us
    concatenate x1, other arithmetic, on_device(): jnp.concatenate([dilated_weight.reshape(-1, channels), mixing_weight], ax...  0.96 us
    select_n x1, other arithmetic, on_device(): jnp.where(to % 2 == 0, trunk[None, :, :half], trunk[None, :, half:])  0.87 us
  transfers between devices with their start and end apart: 2, of which 1 were waited for; matrix products, arithmetic and copies ran while one was open for 5% of the time, Pallas kernels for 0%

profile of v2, /device:TPU:0, one launch (start us, length us, event | category | flops | bytes accessed | tf_op | source)
XLA Modules:
  0.0 39.1 jit_solution(9595929281225994116)
XLA Ops:
  0.0 0.7 %fusion.4 = (bf16[32,128]{1,0:T(8,128)(2,1)S(1)}, bf16[32,128]{1,0:T(8,128)(2,1)S(1)}) fusion(bf16[32,256]{1,0:T(8,128)(2,1)} %param.6), kind=kLoop, calls=%fused_computation.10 | loop fusion | bytes 32768 | tf_op jit(solution)/shard_map/slice | solution.py:253
  0.7 0.9 %fusion.2 = bf16[32,32,128]{2,1,0:T(8,128)(2,1)} fusion(s32[32]{0:T(128)S(1)} %get-tuple-element.7, s32[32]{0:T(128)S(1)} %get-tuple-element.8, pred[32]{0:T(512)(128)(4,1)S(1)} %compare_and_fusion, bf16[32,128]{1,0:T(8,128)(2,1)S(1)} %get-tuple-element.6, bf16[32,128]{1,0:T(8,128)(2,1)S(1)} %get-tuple-element.5), kind=kLoop, calls=%fused_computation.5 | loop fusion | flops 393216 | bytes 278816 | tf_op jit(solution)/shard_map/jit(_where)/select_n | solution.py:253
  1.6 7.3 %all-to-all-start = ((bf16[32,32,128]{2,1,0:T(8,128)(2,1)}), bf16[32,32,128]{2,1,0:T(8,128)(2,1)S(1)}, u32[]{:S(2)}, u32[]{:S(2)}) async-start(bf16[32,32,128]{2,1,0:T(8,128)(2,1)} %fusion.2), calls=%async_computation | async-start | bytes 524288 | tf_op jit(solution)/shard_map/all_to_all | solution.py:254
  8.9 1.0 %fusion.3 = bf16[480,512]{1,0:T(8,128)(2,1)S(1)} fusion(bf16[48,48]{1,0:T(8,128)(2,1)} %param.11, bf16[432,48]{1,0:T(8,128)(2,1)} %bitcast.5), kind=kLoop, calls=%fused_computation.6 | loop fusion | flops 1720320 | bytes 537600 | tf_op jit(solution)/shard_map/concatenate | solution.py:247
  9.9 9.4 %all-to-all-done = bf16[32,32,128]{2,1,0:T(8,128)(2,1)S(1)} async-done(((bf16[32,32,128]{2,1,0:T(8,128)(2,1)}), bf16[32,32,128]{2,1,0:T(8,128)(2,1)S(1)}, u32[]{:S(2)}, u32[]{:S(2)}) %all-to-all-start) | async-done | bytes 262176 | tf_op jit(solution)/shard_map/all_to_all | solution.py:254
  19.3 0.4 collective-permute-start
  19.7 1.1 %pad_maximum_fusion.weights = bf16[1040,512]{1,0:T(8,128)(2,1)S(1)} fusion(bf16[480,512]{1,0:T(8,128)(2,1)S(1)} %fusion.3, bf16[48,512]{1,0:T(8,128)(2,1)} %bitcast.6, bf16[256,512]{1,0:T(8,128)(2,1)} %param.8, bf16[256,512]{1,0:T(8,128)(2,1)} %param.7), kind=kLoop, calls=%fused_computation | loop fusion | flops 4259840 | bytes 2129920 | tf_op jit(solution)/shard_map/concatenate | solution.py:249
  20.8 0.0 collective-permute-done.other
  20.8 18.3 %pair_block.1 = bf16[48,256,128]{2,1,0:T(8,128)(2,1)} custom-call(bf16[1024,128]{1,0:T(8,128)(2,1)S(1)} %bitcast.4, bf16[1024,128]{1,0:T(8,128)(2,1)S(1)} %collective-permute-done.other, bf16[1040,512]{1,0:T(8,128)(2,1)S(1)} %pad_maximum_fusion.weights), custom_call_target="tpu_custom_call" | custom-call | tf_op jit(solution)/shard_map/pair_block/pallas_call | solution.py:259
  (2 shorter events, 0.0 us)
Async XLA Ops:
  1.6 17.7 %all-to-all-start = ((bf16[32,32,128]{2,1,0:T(8,128)(2,1)}), bf16[32,32,128]{2,1,0:T(8,128)(2,1)S(1)}, u32[]{:S(2)}, u32[]{:S(2)}) async-start(bf16[32,32,128]{2,1,0:T(8,128)(2,1)} %fusion.2), calls=%async_computation | async-start | bytes 524288 | tf_op jit(solution)/shard_map/all_to_all | solution.py:254
  19.3 1.5 %collective-permute-start = (bf16[1024,128]{1,0:T(8,128)(2,1)S(1)}, bf16[1024,128]{1,0:T(8,128)(2,1)S(1)}, u32[]{:S(2)}, u32[]{:S(2)}) collective-permute-start(bf16[1024,128]{1,0:T(8,128)(2,1)S(1)} %bitcast.3), channel_id=1, source_target_pairs={{0,1},{1,0},{2,3},{3,2},{4,5},{5,4},{6,7},{7,6},{8,9},{9,8},{10,11... | collective-permute-start | bytes 786440 | tf_op jit(solution)/shard_map/ppermute | solution.py:255
